TPU v7x, 32 devices: a whole 2x2x4 slice. The times are simulated.
32 devices in a mesh: parts: 2 (over x), scan: 16 (over z, y, core).
Axes of the slice: x: 2, y: 2, z: 4, core: 2. Of those that a mesh axis runs over, the one named last changes fastest.
Arguments:
- object_slices: float32 [4, 2, 4096, 256], P('parts', None, 'scan'), parts along dimension 0, may hold values from -4 to 4
- probe_modes: float32 [8, 2, 128, 128], P('parts'), parts along dimension 0, may hold values from -4 to 4
- propagator_phase: float32 [128, 128], replicated, may hold values from -3.140625 to 3.140625
- measured: float32 [256, 128, 128], P(('parts', 'scan')), parts along dimension 0, may hold values from 0.5 to 3
- positions: int32 [256, 2], P(('parts', 'scan')), parts along dimension 0, may hold values from 0 to 3839, as said below
- live_count: int32 [32], P(('parts', 'scan')), parts along dimension 0, may hold values from 1 to 8, as said below
Outputs:
- object_gradient: float32 [4, 2, 4096, 256], P('parts', None, 'scan'), parts along dimension 0
- probe_gradient: float32 [8, 2, 128, 128], P('parts'), parts along dimension 0
- position_loss: float32 [256], P(('parts', 'scan')), parts along dimension 0
There are 2 independent parts, one for each index of `parts`. A program takes and returns all parts, laid end to end along the dimension named above; an argument that names none is the same for every part. Nothing has to cross between parts.
Inputs may be any that keep to these rules, and one draw needn't show every extreme that they name: `positions`: object tile k is rows k * 256 to (k + 1) * 256 - 1. Slots s * 8 to (s + 1) * 8 - 1 belong to scan owner s; each of their windows lies within tiles s - 2 to s + 2 and never in the last tile alone; columns start at 0 to 128. Every owner has a slot in tile max(s - 2, 0) and a slot whose window reaches tile min(s + 2, 16 - 1). `live_count`: live slots of an owner come first; some owner is full in every draw.
All inputs are finite; a program needn't handle non-finite values.
Results may differ from a plain program's by a relative error of at most 0.0003.
Values sent between devices are 32-bit elements; how exact they have to be, the bound alone decides.
No kernel may reach another device: no remote copies, remote signals or barrier semaphores. Data moves between devices by JAX's collectives and lax.ppermute only.
A program may use at most 128 MiB of HBM per device.

v0:
```python
import math

import jax
import jax.numpy as jnp
from jax import lax
from jax.sharding import PartitionSpec as P

REACH = 2


def from_behind(value, axis, steps):
    count = lax.axis_size(axis)
    first, last = (max(0, -steps), min(count, count - steps))
    return lax.ppermute(value, axis, [(source, source + steps) for source in range(first, last)])


def fourier_tables(size):
    counter = jnp.arange(size, dtype=jnp.int32)
    turns = counter[:, None] * counter[None, :] % size
    angles = turns.astype(jnp.float32) * (2.0 * math.pi / size)
    factor = 1.0 / math.sqrt(size)
    return (jnp.cos(angles) * factor, jnp.sin(angles) * -factor)


def left_product(table, values):
    return jnp.einsum("jk,mkl->mjl", table, values, precision=lax.Precision.HIGHEST)


def right_product(values, table):
    return jnp.einsum("mjk,kl->mjl", values, table, precision=lax.Precision.HIGHEST)


def transform(table_real, table_imag, wave_real, wave_imag):
    inner_real = left_product(table_real, wave_real) - left_product(table_imag, wave_imag)
    inner_imag = left_product(table_real, wave_imag) + left_product(table_imag, wave_real)
    outer_real = right_product(inner_real, table_real) - right_product(inner_imag, table_imag)
    outer_imag = right_product(inner_real, table_imag) + right_product(inner_imag, table_real)
    return (outer_real, outer_imag)


def slot_loss(cell_values, mode_values, prop_real, prop_imag, target, table_real, table_imag):
    wave_real = mode_values[:, 0]
    wave_imag = mode_values[:, 1]
    for depth in range(cell_values.shape[0]):
        if depth > 0:
            spec_real, spec_imag = transform(table_real, table_imag, wave_real, wave_imag)
            moved_real = spec_real * prop_real - spec_imag * prop_imag
            moved_imag = spec_real * prop_imag + spec_imag * prop_real
            wave_real, wave_imag = transform(table_real, -table_imag, moved_real, moved_imag)
        trans_real = cell_values[depth, 0]
        trans_imag = cell_values[depth, 1]
        wave_real, wave_imag = (
            wave_real * trans_real - wave_imag * trans_imag,
            wave_real * trans_imag + wave_imag * trans_real,
        )
    far_real, far_imag = transform(table_real, table_imag, wave_real, wave_imag)
    intensity = jnp.sum(far_real * far_real + far_imag * far_imag, axis=0)
    amplitude = jnp.sqrt(intensity + 0.5)
    residual_cells = amplitude - target
    return 0.5 * jnp.sum(residual_cells * residual_cells)


def cut_windows(source, wanted, top_row, patch_size):
    highest = source.shape[2] - patch_size
    anchor = jnp.zeros((), jnp.int32)

    def window(position):
        start = jnp.clip(position[0] - top_row, 0, highest)
        corner = (anchor, anchor, start, position[1])
        return lax.dynamic_slice(
            source, corner, (source.shape[0], source.shape[1], patch_size, patch_size)
        )

    return jax.vmap(window)(wanted)


def add_windows(target, pieces, wanted, top_row, patch_size):
    highest = target.shape[2] - patch_size
    anchor = jnp.zeros((), jnp.int32)
    extent = (target.shape[0], target.shape[1], patch_size, patch_size)

    def add_one(slot_id, current):
        position = wanted[slot_id]
        start = jnp.clip(position[0] - top_row, 0, highest)
        corner = (anchor, anchor, start, position[1])
        block = lax.dynamic_slice(current, corner, extent)
        return lax.dynamic_update_slice(current, block + pieces[slot_id], corner)

    return lax.fori_loop(0, wanted.shape[0], add_one, target)


def shards(object_slices, probe_modes, propagator_phase, measured, positions, live_count):
    patch_size = probe_modes.shape[-1]
    tile_rows = object_slices.shape[2]
    slot_count = positions.shape[0]
    table_real, table_imag = fourier_tables(patch_size)
    prop_real = jnp.cos(propagator_phase)
    prop_imag = jnp.sin(propagator_phase)
    tile_top = lax.axis_index("scan") * tile_rows
    padded = jnp.pad(object_slices, ((0, 0), (0, 0), (patch_size, patch_size), (0, 0)))
    window_top = tile_top - patch_size
    requests = []
    patches = jnp.zeros(
        (slot_count, object_slices.shape[0], 2, patch_size, patch_size), jnp.float32
    )
    for offset in range(-REACH, REACH + 1):
        if offset == 0:
            wanted = positions
        else:
            wanted = from_behind(positions, "scan", offset)
        requests.append(wanted)
        pieces = cut_windows(padded, wanted, window_top, patch_size)
        if offset == 0:
            arrived = pieces
        else:
            arrived = from_behind(pieces, "scan", -offset)
        patches = patches + arrived
    live_slots = live_count[0]

    def one_slot(slot_id, carry):
        grads, losses, mode_total = carry
        cells = patches[slot_id]
        target = measured[slot_id]

        def local_loss(cell_values, mode_values):
            return slot_loss(
                cell_values, mode_values, prop_real, prop_imag, target, table_real, table_imag
            )

        loss_value, pullback = jax.vjp(local_loss, cells, probe_modes)
        cell_grad, mode_grad = pullback(jnp.ones_like(loss_value))
        grads = grads.at[slot_id].set(cell_grad)
        losses = losses.at[slot_id].set(loss_value * (2.0 / (patch_size * patch_size)))
        return (grads, losses, mode_total + mode_grad)

    start_state = (
        jnp.zeros_like(patches),
        jnp.zeros((slot_count,), jnp.float32),
        jnp.zeros_like(probe_modes),
    )
    grads, position_loss, mode_total = lax.fori_loop(0, live_slots, one_slot, start_state)
    probe_gradient = lax.psum(mode_total, "scan")
    grad_padded = jnp.zeros_like(padded)
    for offset in range(-REACH, REACH + 1):
        if offset == 0:
            returned = grads
        else:
            returned = from_behind(grads, "scan", offset)
        grad_padded = add_windows(
            grad_padded, returned, requests[offset + REACH], window_top, patch_size
        )
    object_gradient = grad_padded[:, :, patch_size : patch_size + tile_rows]
    return (object_gradient, probe_gradient, position_loss)


def solution(mesh):
    return jax.shard_map(
        shards,
        mesh=mesh,
        in_specs=(
            P("parts", None, "scan", None),
            P("parts", None, None, None),
            P(),
            P(("parts", "scan"), None, None),
            P(("parts", "scan"), None),
            P(("parts", "scan")),
        ),
        out_specs=(
            P("parts", None, "scan", None),
            P("parts", None, None, None),
            P(("parts", "scan")),
        ),
        check_vma=False,
    )
```

profile of v0, /device:TPU:18, one launch (start us, length us, event | category | flops | bytes accessed | tf_op | source)
XLA Modules:
  0.0 971.2 jit_solution(15926074502137323683)
XLA Ops:
  24.1 23.2 %while.95 = (s32[]{:T(128)}, f32[2,2,512,256]{3,2,1,0:T(8,128)S(1)}, s32[8,4]{0,1:T(4,128)S(1)}, f32[8,2,2,128,128]{4,3,2,1,0:T(8,128)}, s32[]{:T(128)}) while((s32[]{:T(128)}, f32[2,2,512,256]{3,2,1,0:T(8,128)S(1)}, s32[8,4]{0,1:T(4,128)S(1)}, f32[8,2,2,128,128]{4,3,2,1,0:T(8,128)}, s32[]{:T(128)}) %tuple.310), condition=%wide.while_cond.2, body=%wide.while_body.2.sunk | while | flops 2 | bytes 525937 | solution.py:70
  47.3 3.7 collective-permute-start.1
  52.6 22.0 %while.96 = (s32[]{:T(128)}, f32[2,2,512,256]{3,2,1,0:T(8,128)S(1)}, s32[8,4]{0,1:T(4,128)S(1)}, f32[8,2,2,128,128]{4,3,2,1,0:T(8,128)}, s32[]{:T(128)}) while((s32[]{:T(128)}, f32[2,2,512,256]{3,2,1,0:T(8,128)S(1)}, s32[8,4]{0,1:T(4,128)S(1)}, f32[8,2,2,128,128]{4,3,2,1,0:T(8,128)}, s32[]{:T(128)}) %tuple.337), condition=%wide.while_cond.3, body=%wide.while_body.3.sunk | while | flops 2 | bytes 525937 | solution.py:70
  78.8 22.7 %while.98 = (s32[]{:T(128)}, f32[2,2,512,256]{3,2,1,0:T(8,128)S(1)}, s32[8,4]{0,1:T(4,128)S(1)}, f32[8,2,2,128,128]{4,3,2,1,0:T(8,128)}, s32[]{:T(128)}) while((s32[]{:T(128)}, f32[2,2,512,256]{3,2,1,0:T(8,128)S(1)}, s32[8,4]{0,1:T(4,128)S(1)}, f32[8,2,2,128,128]{4,3,2,1,0:T(8,128)}, s32[]{:T(128)}) %tuple.338), condition=%wide.while_cond.5, body=%wide.while_body.5.sunk | while | flops 2 | bytes 525937 | solution.py:70
  101.4 3.8 collective-permute-start.5
  106.8 21.4 %while.99 = (s32[]{:T(128)}, f32[2,2,512,256]{3,2,1,0:T(8,128)S(1)}, s32[8,4]{0,1:T(4,128)S(1)}, f32[8,2,2,128,128]{4,3,2,1,0:T(8,128)}, s32[]{:T(128)}) while((s32[]{:T(128)}, f32[2,2,512,256]{3,2,1,0:T(8,128)S(1)}, s32[8,4]{0,1:T(4,128)S(1)}, f32[8,2,2,128,128]{4,3,2,1,0:T(8,128)}, s32[]{:T(128)}) %tuple.339), condition=%wide.while_cond.6, body=%wide.while_body.6.sunk | while | flops 2 | bytes 525937 | solution.py:70
  131.9 21.9 %while.97 = (s32[]{:T(128)}, f32[2,2,512,256]{3,2,1,0:T(8,128)S(1)}, s32[8,4]{0,1:T(4,128)S(1)}, f32[8,2,2,128,128]{4,3,2,1,0:T(8,128)}, s32[]{:T(128)}) while((s32[]{:T(128)}, f32[2,2,512,256]{3,2,1,0:T(8,128)S(1)}, s32[8,4]{0,1:T(4,128)S(1)}, f32[8,2,2,128,128]{4,3,2,1,0:T(8,128)}, s32[]{:T(128)}) %tuple.340), condition=%wide.while_cond.4, body=%wide.while_body.4.sunk | while | flops 2 | bytes 525937 | solution.py:70
  153.8 34.9 %collective-permute-done.7 = f32[8,2,2,128,128]{4,3,2,1,0:T(8,128)} collective-permute-done((f32[8,2,2,128,128]{4,3,2,1,0:T(8,128)}, f32[8,2,2,128,128]{4,3,2,1,0:T(8,128)}, u32[]{:S(2)}, u32[]{:S(2)}) %collective-permute-start.7) | collective-permute-done | bytes 2097184 | tf_op jit(solution)/shard_map/ppermute | solution.py:14
  188.8 6.7 add_add_fusion.1
  197.1 152.0 %while.100 = (s32[]{:T(128)}, f32[8,2,2,128,128]{4,3,2,1,0:T(8,128)}, f32[8]{0:T(128)S(1)}, f32[4,2,128,128]{2,3,0,1:T(8,128)S(1)}, s32[]{:T(128)}, /*index=5*/f...) while((s32[]{:T(128)}, ...), condition=%wide.region_12.13_spmd.clone.clone, body=%wide.region_0.12_spmd.clone.clone.sunk | while | flops 4852858880 | bytes 47580520 | solution.py:141
  349.1 209.2 %collective-permute-start.8 = (f32[8,2,2,128,128]{4,3,2,1,0:T(8,128)}, f32[8,2,2,128,128]{4,3,2,1,0:T(8,128)}, u32[]{:S(2)}, u32[]{:S(2)}) collective-permute-start(f32[8,2,2,128,128]{4,3,2,1,0:T(8,128)} %get-tuple-element.1804), channel_id=1, source_target_pairs={{2,0},{3,1},{4,2},{5,3},{6,4},{7,5},{8,6},{9,7},{10,8},{11,9},{12,... | collective-permute-start | bytes 6291464 | tf_op jit(solution)/shard_map/ppermute | solution.py:14
  565.7 95.0 %collective-permute-done.8 = f32[8,2,2,128,128]{4,3,2,1,0:T(8,128)} collective-permute-done((f32[8,2,2,128,128]{4,3,2,1,0:T(8,128)}, f32[8,2,2,128,128]{4,3,2,1,0:T(8,128)}, u32[]{:S(2)}, u32[]{:S(2)}) %collective-permute-start.8) | collective-permute-done | bytes 2097184 | tf_op jit(solution)/shard_map/ppermute | solution.py:14
  660.9 59.2 %while.90 = (s32[]{:T(128)}, f32[2,2,512,256]{3,2,1,0:T(8,128)S(1)}, s32[8,2]{0,1:T(2,128)S(1)}, s32[]{:T(128)}, f32[8,2,2,128,128]{4,3,2,1,0:T(8,128)}, /*index=5*/s32[]{:T(128)}, s32[]{:T(128)}, s32[]{:T(128)}, s32[]{:T(128)}) while((s32[]{:T(128)}, f32[2,2,512,256]{3,2,1,0:T(8,128)S(1)}, s32[8,2]{0,1:T(2,128)S(1)}, s32[]{:T(128)}, ...), condition=%wide.region_14.15_spmd, body=%wide.region_13.14_spmd.sunk | while | flops 65544 | bytes 1310935 | solution.py:89
  720.1 60.0 %while.91 = (s32[]{:T(128)}, f32[2,2,512,256]{3,2,1,0:T(8,128)S(1)}, s32[8,2]{0,1:T(2,128)S(1)}, s32[]{:T(128)}, f32[8,2,2,128,128]{4,3,2,1,0:T(8,128)}, /*index=5*/s32[]{:T(128)}, s32[]{:T(128)}, s32[]{:T(128)}, s32[]{:T(128)}) while((s32[]{:T(128)}, f32[2,2,512,256]{3,2,1,0:T(8,128)S(1)}, s32[8,2]{0,1:T(2,128)S(1)}, s32[]{:T(128)}, ...), condition=%wide.region_16.17_spmd, body=%wide.region_15.16_spmd.sunk | while | flops 65544 | bytes 1310935 | solution.py:89
  724.5 3.4 dynamic_update_slice.41
  754.1 3.4 dynamic_update_slice.41
  769.1 3.4 dynamic_update_slice.41
  780.2 59.3 %while.92 = (s32[]{:T(128)}, f32[2,2,512,256]{3,2,1,0:T(8,128)S(1)}, s32[8,2]{0,1:T(2,128)S(1)}, s32[]{:T(128)}, f32[8,2,2,128,128]{4,3,2,1,0:T(8,128)}, /*index=5*/s32[]{:T(128)}, s32[]{:T(128)}, s32[]{:T(128)}, s32[]{:T(128)}) while((s32[]{:T(128)}, f32[2,2,512,256]{3,2,1,0:T(8,128)S(1)}, s32[8,2]{0,1:T(2,128)S(1)}, s32[]{:T(128)}, ...), condition=%wide.region_18.19_spmd, body=%wide.region_17.18_spmd.sunk | while | flops 65544 | bytes 1310935 | solution.py:89
  791.2 3.4 dynamic_update_slice.42
  798.7 3.4 dynamic_update_slice.42
  806.2 3.4 dynamic_update_slice.42
  813.6 3.4 dynamic_update_slice.42
  821.1 3.4 dynamic_update_slice.42
  828.6 3.4 dynamic_update_slice.42
  839.5 59.0 %while.93 = (s32[]{:T(128)}, f32[2,2,512,256]{3,2,1,0:T(8,128)S(1)}, s32[8,2]{0,1:T(2,128)S(1)}, s32[]{:T(128)}, f32[8,2,2,128,128]{4,3,2,1,0:T(8,128)}, /*index=5*/s32[]{:T(128)}, s32[]{:T(128)}, s32[]{:T(128)}, s32[]{:T(128)}) while((s32[]{:T(128)}, f32[2,2,512,256]{3,2,1,0:T(8,128)S(1)}, s32[8,2]{0,1:T(2,128)S(1)}, s32[]{:T(128)}, ...), condition=%wide.region_20.21_spmd, body=%wide.region_19.20_spmd.sunk | while | flops 65544 | bytes 1310935 | solution.py:89
  843.5 3.4 dynamic_update_slice.43
  895.1 3.4 dynamic_update_slice.43
  898.5 62.8 %while.94 = (s32[]{:T(128)}, f32[2,2,512,256]{3,2,1,0:T(8,128)S(1)}, s32[8,2]{0,1:T(2,128)S(1)}, s32[]{:T(128)}, f32[8,2,2,128,128]{4,3,2,1,0:T(8,128)}, /*index=5*/s32[]{:T(128)}, s32[]{:T(128)}, s32[]{:T(128)}, s32[]{:T(128)}) while((s32[]{:T(128)}, f32[2,2,512,256]{3,2,1,0:T(8,128)S(1)}, s32[8,2]{0,1:T(2,128)S(1)}, s32[]{:T(128)}, ...), condition=%wide.region_22.23_spmd, body=%wide.region_21.22_spmd.sunk | while | flops 65544 | bytes 1310935 | solution.py:89
  934.3 3.4 dynamic_update_slice.44
  942.2 3.4 dynamic_update_slice.44
  950.0 3.4 dynamic_update_slice.44
  957.8 3.4 dynamic_update_slice.44
  (508 shorter events, 417.5 us)
Async XLA Ops:
  7.2 955.2 %all-reduce.9.cloned.1.call-start = ((), (), s32[]{:S(2)}) async-start(), calls=%async_computation | async-start | bytes 1048576 | tf_op jit(solution)/shard_map/psum | solution.py:142
  7.2 15.0 %collective-permute-start.2 = (s32[8,2]{0,1:T(2,128)}, s32[8,2]{0,1:T(2,128)S(1)}, u32[]{:S(2)}, u32[]{:S(2)}) collective-permute-start(s32[8,2]{0,1:T(2,128)} %param.26), channel_id=1, source_target_pairs={{1,0},{2,1},{3,2},{4,3},{5,4},{6,5},{7,6},{8,7},{9,8},{10,9},{11,1... | collective-permute-start | bytes 200 | tf_op jit(solution)/shard_map/ppermute | solution.py:14
  10.0 12.3 %collective-permute-start = (s32[8,2]{0,1:T(2,128)}, s32[8,2]{0,1:T(2,128)S(1)}, u32[]{:S(2)}, u32[]{:S(2)}) collective-permute-start(s32[8,2]{0,1:T(2,128)} %param.26), channel_id=1, source_target_pairs={{2,0},{3,1},{4,2},{5,3},{6,4},{7,5},{8,6},{9,7},{10,8},{11,9},{12,... | collective-permute-start | bytes 200 | tf_op jit(solution)/shard_map/ppermute | solution.py:14
  12.5 9.8 %collective-permute-start.4 = (s32[8,2]{0,1:T(2,128)}, s32[8,2]{0,1:T(2,128)S(1)}, u32[]{:S(2)}, u32[]{:S(2)}) collective-permute-start(s32[8,2]{0,1:T(2,128)} %param.26), channel_id=1, source_target_pairs={{0,1},{1,2},{2,3},{3,4},{4,5},{5,6},{6,7},{7,8},{8,9},{9,10},{10,1... | collective-permute-start | bytes 200 | tf_op jit(solution)/shard_map/ppermute | solution.py:14
  14.6 7.7 collective-permute-start.6
  47.3 106.5 %collective-permute-start.1 = (f32[8,2,2,128,128]{4,3,2,1,0:T(8,128)}, f32[8,2,2,128,128]{4,3,2,1,0:T(8,128)}, u32[]{:S(2)}, u32[]{:S(2)}) collective-permute-start(f32[8,2,2,128,128]{4,3,2,1,0:T(8,128)} %get-tuple-element.807), channel_id=1, source_target_pairs={{0,2},{1,3},{2,4},{3,5},{4,6},{5,7},{6,8},{7,9},{8,10},{9,11},{10,... | collective-permute-start | bytes 6291464 | tf_op jit(solution)/shard_map/ppermute | solution.py:14
  74.5 79.3 %collective-permute-start.3 = (f32[8,2,2,128,128]{4,3,2,1,0:T(8,128)}, f32[8,2,2,128,128]{4,3,2,1,0:T(8,128)}, u32[]{:S(2)}, u32[]{:S(2)}) collective-permute-start(f32[8,2,2,128,128]{4,3,2,1,0:T(8,128)} %get-tuple-element.815), channel_id=1, source_target_pairs={{0,1},{1,2},{2,3},{3,4},{4,5},{5,6},{6,7},{7,8},{8,9},{9,10},{10,1... | collective-permute-start | bytes 6291464 | tf_op jit(solution)/shard_map/ppermute | solution.py:14
  101.4 52.4 %collective-permute-start.5 = (f32[8,2,2,128,128]{4,3,2,1,0:T(8,128)}, f32[8,2,2,128,128]{4,3,2,1,0:T(8,128)}, u32[]{:S(2)}, u32[]{:S(2)}) collective-permute-start(f32[8,2,2,128,128]{4,3,2,1,0:T(8,128)} %get-tuple-element.831), channel_id=1, source_target_pairs={{1,0},{2,1},{3,2},{4,3},{5,4},{6,5},{7,6},{8,7},{9,8},{10,9},{11,1... | collective-permute-start | bytes 6291464 | tf_op jit(solution)/shard_map/ppermute | solution.py:14
  128.2 60.6 %collective-permute-start.7 = (f32[8,2,2,128,128]{4,3,2,1,0:T(8,128)}, f32[8,2,2,128,128]{4,3,2,1,0:T(8,128)}, u32[]{:S(2)}, u32[]{:S(2)}) collective-permute-start(f32[8,2,2,128,128]{4,3,2,1,0:T(8,128)} %get-tuple-element.839), channel_id=1, source_target_pairs={{2,0},{3,1},{4,2},{5,3},{6,4},{7,5},{8,6},{9,7},{10,8},{11,9},{12,... | collective-permute-start | bytes 6291464 | tf_op jit(solution)/shard_map/ppermute | solution.py:14
  195.4 1.6 copy-start.2
  349.1 311.8 %copy-start.1 = (f32[8]{0:T(128)}, f32[8]{0:T(128)S(1)}, u32[]{:S(2)}) copy-start(f32[8]{0:T(128)S(1)} %get-tuple-element.1883) | copy-start | bytes 100
  349.1 311.6 %collective-permute-start.8 = (f32[8,2,2,128,128]{4,3,2,1,0:T(8,128)}, f32[8,2,2,128,128]{4,3,2,1,0:T(8,128)}, u32[]{:S(2)}, u32[]{:S(2)}) collective-permute-start(f32[8,2,2,128,128]{4,3,2,1,0:T(8,128)} %get-tuple-element.1804), channel_id=1, source_target_pairs={{2,0},{3,1},{4,2},{5,3},{6,4},{7,5},{8,6},{9,7},{10,8},{11,9},{12,... | collective-permute-start | bytes 6291464 | tf_op jit(solution)/shard_map/ppermute | solution.py:14
  558.3 161.8 %collective-permute-start.9 = (f32[8,2,2,128,128]{4,3,2,1,0:T(8,128)}, f32[8,2,2,128,128]{4,3,2,1,0:T(8,128)}, u32[]{:S(2)}, u32[]{:S(2)}) collective-permute-start(f32[8,2,2,128,128]{4,3,2,1,0:T(8,128)} %get-tuple-element.1804), channel_id=1, source_target_pairs={{1,0},{2,1},{3,2},{4,3},{5,4},{6,5},{7,6},{8,7},{9,8},{10,9},{11,1... | collective-permute-start | bytes 6291464 | tf_op jit(solution)/shard_map/ppermute | solution.py:14
  560.2 279.3 %collective-permute-start.10 = (f32[8,2,2,128,128]{4,3,2,1,0:T(8,128)}, f32[8,2,2,128,128]{4,3,2,1,0:T(8,128)}, u32[]{:S(2)}, u32[]{:S(2)}) collective-permute-start(f32[8,2,2,128,128]{4,3,2,1,0:T(8,128)} %get-tuple-element.1804), channel_id=1, source_target_pairs={{0,1},{1,2},{2,3},{3,4},{4,5},{5,6},{6,7},{7,8},{8,9},{9,10},{10,1... | collective-permute-start | bytes 6291464 | tf_op jit(solution)/shard_map/ppermute | solution.py:14
  562.6 335.9 %collective-permute-start.11 = (f32[8,2,2,128,128]{4,3,2,1,0:T(8,128)}, f32[8,2,2,128,128]{4,3,2,1,0:T(8,128)}, u32[]{:S(2)}, u32[]{:S(2)}) collective-permute-start(f32[8,2,2,128,128]{4,3,2,1,0:T(8,128)} %get-tuple-element.1804), channel_id=1, source_target_pairs={{0,2},{1,3},{2,4},{3,5},{4,6},{5,7},{6,8},{7,9},{8,10},{9,11},{10,... | collective-permute-start | bytes 6291464 | tf_op jit(solution)/shard_map/ppermute | solution.py:14
  720.1 60.1 %copy-start = (s32[8,2]{0,1:T(2,128)S(1)}, s32[8,2]{0,1:T(2,128)}, u32[]{:S(2)}) copy-start(s32[8,2]{0,1:T(2,128)} %param.26) | copy-start | bytes 196
Sparse Core Ops, SparseCore 0:
  565.8 140.1 all-reduce.8
where the time goes:
time: 987 us; the launch traced here: 971 us
  local copies, waits for them, and re-layouts  289 us (29%)
  starting transfers between devices  238 us (24%)
  loops' own time  135 us (14%)
  waiting for transfers between devices  130 us (13%)
  matrix products  99 us (10%)
  other arithmetic  66.2 us (7%)
  between operations  14.5 us (1%)
    ppermute x12, starting transfers between devices, from_behind(): lax.ppermute(value, axis, [(source, source + steps) for source in range(f...  238 us
    ppermute x12, waiting for transfers between devices, from_behind(): lax.ppermute(value, axis, [(source, source + steps) for source in range(f...  130 us
    dynamic_update_slice x40, local copies, waits for them, and re-layouts, add_one(): return lax.dynamic_update_slice(current, block + pieces[slot_id], corner)  130 us
    gather x120, local copies, waits for them, and re-layouts  111 us
    another operation x5, loops' own time, add_windows(): return lax.fori_loop(0, wanted.shape[0], add_one, target)  101 us
    dot_general x72, matrix products, left_product(): jnp.einsum('jk,mkl->mjl', table, values, precision=lax.Precision.HIGHEST)  50.6 us
    dot_general x72, matrix products, right_product(): jnp.einsum('mjk,kl->mjl', values, table, precision=lax.Precision.HIGHEST)  48.4 us
    add x40, other arithmetic, add_one(): return lax.dynamic_update_slice(current, block + pieces[slot_id], corner)  43.9 us
  transfers between devices with their start and end apart: 13, of which 2 were waited for; matrix products, arithmetic and copies ran while one was open for 31% of the time, Pallas kernels for 0%

commit v1 on v0

v1 whole, which is shorter than its diff:
```python
import functools
import math

import jax
import jax.numpy as jnp
import numpy as np
from jax import lax
from jax.experimental import pallas as pl
from jax.experimental.pallas import tpu as pltpu
from jax.sharding import PartitionSpec as P

F32 = jnp.float32
BF16 = jnp.bfloat16
LOSS_PAD = 32


def shifted(value, axis, steps):
    count = lax.axis_size(axis)
    first, last = (max(0, -steps), min(count, count - steps))
    return lax.ppermute(value, axis, [(source, source + steps) for source in range(first, last)])


def swapped(value, axis, bit):
    count = lax.axis_size(axis)
    return lax.ppermute(value, axis, [(source, source ^ bit) for source in range(count)])


def tables(size):
    counter = np.arange(size)
    angles = (counter[:, None] * counter[None, :] % size) * (2.0 * math.pi / size)
    cosine = np.cos(angles) / math.sqrt(size)
    sine = np.sin(angles) / math.sqrt(size)
    forward = np.block([[cosine, -sine], [sine, cosine]]).astype(np.float32)
    high = forward.astype(jnp.bfloat16)
    low = (forward - high.astype(np.float32)).astype(jnp.bfloat16)
    right_f = np.concatenate([high, high, low], 0)
    right_g = np.concatenate([high.T, high.T, low.T], 0)
    left_f = np.concatenate([high.T, high.T, low.T], 1)
    left_g = np.concatenate([high, high, low], 1)
    return right_f, right_g, left_f, left_g


def kernel(
    size, modes, slots, tile, place_ref, slot_ref, own_ref, pair_ref, pats, wave_ref, prop_ref,
    rf_ref, rg_ref, lf_ref, lg_ref, mine_ref, theirs_ref, modegrad_ref,
    obj, acc, pat, cells, cgrad, wave1, far, ops, sem,
):
    core = place_ref[0]
    chip_top = place_ref[1]
    first_id = place_ref[2]
    half = size // 2
    top = lax.mul(core, tile)
    other = tile - top
    top = pl.multiple_of(top, tile)
    other = pl.multiple_of(other, tile)

    copies = []

    def move(source, target):
        copy = pltpu.make_async_copy(source, target, sem.at[len(copies)])
        copy.start()
        copies.append(copy)

    rows = slots * size
    (own_pat, pair_pat, up_own, up_pair, down_own, down_pair) = pats
    move(own_ref, obj.at[:, :, pl.ds(top, tile)])
    move(pair_ref, obj.at[:, :, pl.ds(other, tile)])
    for group, (a, b) in enumerate(((up_own, up_pair), (own_pat, pair_pat), (down_own, down_pair))):
        move(a.at[pl.ds(0, rows)], pat.at[2 * group + core])
        move(b.at[pl.ds(0, rows)], pat.at[2 * group + 1 - core])
    halo_row = rows + 8
    for k in range(2):
        for ri in range(2):
            for side in range(2):
                block = pl.ds(halo_row + ((k * 2 + ri) * 2 + side) * half, half)
                lanes = pl.ds(side * size, size)
                move(
                    down_own.at[block],
                    obj.at[k, ri, pl.ds(pl.multiple_of(2 * tile + core * half, half), half), lanes],
                )
                move(
                    down_pair.at[block],
                    obj.at[k, ri, pl.ds(pl.multiple_of(2 * tile + half - core * half, half), half), lanes],
                )
    acc[...] = jnp.zeros_like(acc)
    modegrad_ref[...] = jnp.zeros_like(modegrad_ref)
    for copy in copies:
        copy.wait()

    mat = functools.partial(jnp.dot, preferred_element_type=F32)
    (r1, l1, l2, r2, r3, l3, l4, r4, r5, l5, l6, r6) = range(12)

    def put_right(stage, m, real, imag):
        hi, lo = ops.at[stage, 0], ops.at[stage, 1]
        for part, value in enumerate((real, imag)):
            high = value.astype(BF16)
            at = (pl.ds(m * size, size), pl.ds(part * size, size))
            hi[at] = high
            lo[at] = (value - high.astype(F32)).astype(BF16)

    def right(stage, m, table):
        at = (pl.ds(m * size, size), pl.ds(0, 2 * size))
        high, low = ops.at[stage, 0][at], ops.at[stage, 1][at]
        out = mat(jnp.concatenate([high, low, high], 1), table[...])
        return out[:, :size], out[:, size:]

    def put_left(stage, m, real, imag):
        hi, lo = ops.at[stage, 0], ops.at[stage, 1]
        base = (m // 2) * 2 * size
        for part, value in enumerate((real, imag)):
            high = value.astype(BF16)
            at = (pl.ds(base + part * size, size), pl.ds((m % 2) * size, size))
            hi[at] = high
            lo[at] = (value - high.astype(F32)).astype(BF16)

    def left(stage, p, table):
        at = (pl.ds(p * 2 * size, 2 * size), pl.ds(0, 2 * size))
        high, low = ops.at[stage, 0][at], ops.at[stage, 1][at]
        out = mat(table[...], jnp.concatenate([high, low, high], 0))
        return [(out[:size, j * size:(j + 1) * size], out[size:, j * size:(j + 1) * size]) for j in range(2)]

    def wave_at(m):
        return (wave_ref[m, 0], wave_ref[m, 1])

    def window(slot, row, column):
        base = pl.multiple_of(lax.div(row, 8) * 8, 8)
        ahead = row - base
        tall = size + 8
        for k in range(2):
            for ri in range(2):
                value = obj[k, ri, pl.ds(base, tall), :]
                value = pltpu.roll(value, 2 * size - column, 1)[:, :size]
                cells[k, ri] = pltpu.roll(value, tall - ahead, 0)[:size]
        for m in range(modes):
            pr, pi = wave_at(m)
            o_r, o_i = cells[0, 0], cells[0, 1]
            put_right(r1, m, pr * o_r - pi * o_i, pr * o_i + pi * o_r)
            put_left(l1, m, *right(r1, m, rf_ref))
        for p in range(modes // 2):
            for j, (re, im) in enumerate(left(l1, p, lf_ref)):
                h_r, h_i = prop_ref[0], prop_ref[1]
                put_left(l2, 2 * p + j, re * h_r - im * h_i, re * h_i + im * h_r)
            for j, (re, im) in enumerate(left(l2, p, lg_ref)):
                put_right(r2, 2 * p + j, re, im)
        for m in range(modes):
            re, im = right(r2, m, rg_ref)
            wave1[m, 0] = re
            wave1[m, 1] = im
            o_r, o_i = cells[1, 0], cells[1, 1]
            put_right(r3, m, re * o_r - im * o_i, re * o_i + im * o_r)
            put_left(l3, m, *right(r3, m, rf_ref))
        total = jnp.zeros((size, size), F32)
        for p in range(modes // 2):
            for j, (re, im) in enumerate(left(l3, p, lf_ref)):
                far[2 * p + j, 0] = re
                far[2 * p + j, 1] = im
                total = total + (re * re + im * im)
        target = pat[slot // slots, pl.ds(pl.multiple_of((slot % slots) * size, size), size), :]
        amplitude = jnp.sqrt(total + 0.5)
        residual = amplitude - target
        loss = 0.5 * jnp.sum(residual * residual) * (2.0 / (size * size))
        ratio = residual / amplitude
        at = (pl.ds(2 * modes * size, 8), pl.ds(0, size))
        place = lax.broadcasted_iota(jnp.int32, (8, size), 0) * size + lax.broadcasted_iota(jnp.int32, (8, size), 1)
        modegrad_ref[at] = jnp.where(place == first_id + slot, loss, modegrad_ref[at])
        for p in range(modes // 2):
            for m in (2 * p, 2 * p + 1):
                put_left(l4, m, far[m, 0] * ratio, far[m, 1] * ratio)
            for j, (re, im) in enumerate(left(l4, p, lg_ref)):
                put_right(r4, 2 * p + j, re, im)
        for m in range(modes):
            re, im = right(r4, m, rg_ref)
            w_r, w_i = wave1[m, 0], wave1[m, 1]
            add_r, add_i = re * w_r + im * w_i, im * w_r - re * w_i
            if m == 0:
                cgrad[1, 0] = add_r
                cgrad[1, 1] = add_i
            else:
                cgrad[1, 0] += add_r
                cgrad[1, 1] += add_i
            o_r, o_i = cells[1, 0], cells[1, 1]
            put_right(r5, m, re * o_r + im * o_i, im * o_r - re * o_i)
            put_left(l5, m, *right(r5, m, rf_ref))
        for p in range(modes // 2):
            for j, (re, im) in enumerate(left(l5, p, lf_ref)):
                h_r, h_i = prop_ref[0], prop_ref[1]
                put_left(l6, 2 * p + j, re * h_r + im * h_i, im * h_r - re * h_i)
            for j, (re, im) in enumerate(left(l6, p, lg_ref)):
                put_right(r6, 2 * p + j, re, im)
        for m in range(modes):
            re, im = right(r6, m, rg_ref)
            o_r, o_i = cells[0, 0], cells[0, 1]
            modegrad_ref[pl.ds(2 * m * size, size), :] += re * o_r + im * o_i
            modegrad_ref[pl.ds((2 * m + 1) * size, size), :] += im * o_r - re * o_i
            pr, pi = wave_at(m)
            add_r, add_i = re * pr + im * pi, im * pr - re * pi
            if m == 0:
                cgrad[0, 0] = add_r
                cgrad[0, 1] = add_i
            else:
                cgrad[0, 0] += add_r
                cgrad[0, 1] += add_i
        for k in range(2):
            for ri in range(2):
                value = jnp.concatenate([cgrad[k, ri], jnp.zeros((8, size), F32)], 0)
                value = pltpu.roll(value, ahead, 0)
                value = jnp.concatenate([value, jnp.zeros_like(value)], 1)
                acc[k, ri, pl.ds(base, tall), :] += pltpu.roll(value, column, 1)

    def visit(slot, count):
        row = slot_ref[slot, 0] - chip_top
        here = jnp.logical_and(slot_ref[slot, 2] > 0, jnp.logical_and(row >= 0, row < 2 * tile))

        @pl.when(jnp.logical_and(here, lax.rem(count, 2) == core))
        def _():
            window(slot, row, slot_ref[slot, 1])

        return count + here.astype(jnp.int32)

    lax.fori_loop(0, 6 * slots, visit, jnp.int32(0))

    copies.clear()
    move(acc.at[:, :, pl.ds(top, tile)], mine_ref)
    move(acc.at[:, :, pl.ds(other, tile)], theirs_ref.at[:, :, pl.ds(0, tile)])
    move(acc.at[:, :, pl.ds(2 * tile, size)], theirs_ref.at[:, :, pl.ds(tile, size)])
    for copy in copies:
        copy.wait()


def flat_kernel(size, modes, slots, tile, *refs):
    place_ref, slot_ref, own_ref, pair_ref = refs[:4]
    kernel(size, modes, slots, tile, place_ref, slot_ref, own_ref, pair_ref, refs[4:10], *refs[10:])


def all_windows(place, slot_list, own, pair, pats, waves, prop, slots):
    modes, _, size, _ = waves.shape
    tile = own.shape[2]
    columns = own.shape[3]
    rf, rg, lf, lg = (jnp.asarray(t) for t in tables(size))
    total_rows = 2 * modes * size + LOSS_PAD
    hbm = pl.BlockSpec(memory_space=pl.ANY)
    vmem = pl.BlockSpec(memory_space=pltpu.VMEM)
    smem = pl.BlockSpec(memory_space=pltpu.SMEM)
    return pl.pallas_call(
        functools.partial(flat_kernel, size, modes, slots, tile),
        out_shape=(
            jax.ShapeDtypeStruct((2, 2, tile, columns), F32),
            jax.ShapeDtypeStruct((2, 2, tile + size, columns), F32),
            jax.ShapeDtypeStruct((total_rows, size), F32),
        ),
        in_specs=[smem, smem, hbm, hbm] + [hbm] * 6 + [vmem] * 6,
        out_specs=(hbm, hbm, vmem),
        scratch_shapes=[
            pltpu.VMEM((2, 2, 2 * tile + size, columns), F32),
            pltpu.VMEM((2, 2, 2 * tile + size, columns), F32),
            pltpu.VMEM((6, slots * size, size), F32),
            pltpu.VMEM((2, 2, size, size), F32),
            pltpu.VMEM((2, 2, size, size), F32),
            pltpu.VMEM((modes, 2, size, size), F32),
            pltpu.VMEM((modes, 2, size, size), F32),
            pltpu.VMEM((12, 2, modes * size, 2 * size), BF16),
            pltpu.SemaphoreType.DMA((24,)),
        ],
        compiler_params=pltpu.CompilerParams(vmem_limit_bytes=48 * 1024 * 1024),
    )(place, slot_list, own, pair, *pats, waves, prop, rf, rg, lf, lg)


def sum_over(value, axis):
    count = lax.axis_size(axis)
    index = lax.axis_index(axis)
    bits = [1 << i for i in range(count.bit_length() - 1)]
    split, whole = bits[:2], bits[2:]
    for bit in split:
        half = value.shape[0] // 2
        side = (index // bit) % 2
        kept = lax.dynamic_slice_in_dim(value, side * half, half, 0)
        given = lax.dynamic_slice_in_dim(value, (1 - side) * half, half, 0)
        value = kept + swapped(given, axis, bit)
    for bit in whole:
        value = value + swapped(value, axis, bit)
    for bit in split[::-1]:
        side = (index // bit) % 2
        got = swapped(value, axis, bit)
        value = jnp.concatenate([jnp.where(side == 0, value, got), jnp.where(side == 0, got, value)], 0)
    return value


def shards(object_slices, probe_modes, propagator_phase, measured, positions, live_count):
    modes, _, size, _ = probe_modes.shape
    tile = object_slices.shape[2]
    slots = positions.shape[0]
    index = lax.axis_index("scan")
    core = index % 2
    chip = index // 2
    prop = jnp.stack([jnp.cos(propagator_phase), jnp.sin(propagator_phase)])
    live = jnp.arange(slots, dtype=jnp.int32) < live_count[0]
    facts = jnp.concatenate([positions, live.astype(jnp.int32)[:, None]], 1).astype(F32)
    facts = jnp.pad(facts, ((0, 0), (0, size - 3)))
    own_pat = jnp.concatenate([measured.reshape(slots * size, size), facts], 0)
    up_own = shifted(own_pat, "scan", 2)
    pair = swapped(object_slices, "scan", 1)
    half = size // 2
    first = jnp.where(core == 0, object_slices[:, :, :half], pair[:, :, half:size])
    blocks = [first[k, ri, :, s * size:(s + 1) * size] for k in range(2) for ri in range(2) for s in range(2)]
    down_own = shifted(jnp.concatenate([own_pat] + blocks, 0), "scan", -2)
    pair_pat = swapped(own_pat, "scan", 1)
    up_pair = swapped(up_own, "scan", 1)
    down_pair = swapped(down_own, "scan", 1)
    rows = slots * size
    lists = []
    for a, b in ((up_own, up_pair), (own_pat, pair_pat), (down_own, down_pair)):
        a, b = a[rows:rows + slots, :3], b[rows:rows + slots, :3]
        lists += [jnp.where(core == 0, a, b), jnp.where(core == 0, b, a)]
    slot_list = jnp.concatenate(lists, 0).astype(jnp.int32)
    place = jnp.stack([core, chip * 2 * tile, (chip - 1) * 2 * slots]).astype(jnp.int32)
    mine, theirs, sums = all_windows(
        place, slot_list, object_slices, pair,
        (own_pat, pair_pat, up_own, up_pair, down_own, down_pair), probe_modes, prop, slots,
    )
    back = swapped(theirs, "scan", 1)
    halo = theirs[:, :, tile:] + back[:, :, tile:]
    count = lax.axis_size("scan")
    halo = lax.ppermute(halo, "scan", [(s, s + 1) for s in range(1, count - 1, 2)])
    sums = sum_over(sums, "scan")
    grad = mine + back[:, :, :tile] + jnp.pad(halo, ((0, 0), (0, 0), (0, tile - size), (0, 0)))
    mode_rows = 2 * modes * size
    probe_gradient = sums[:mode_rows].reshape(probe_modes.shape)
    losses = sums[mode_rows:mode_rows + 8].reshape(-1)
    position_loss = lax.dynamic_slice_in_dim(losses, index * slots, slots, 0)
    return (grad, probe_gradient, position_loss)


def solution(mesh):
    return jax.shard_map(
        shards,
        mesh=mesh,
        in_specs=(
            P("parts", None, "scan", None),
            P("parts", None, None, None),
            P(),
            P(("parts", "scan"), None, None),
            P(("parts", "scan"), None),
            P(("parts", "scan")),
        ),
        out_specs=(
            P("parts", None, "scan", None),
            P("parts", None, None, None),
            P(("parts", "scan")),
        ),
        check_vma=False,
    )
```

time: 987 us -> 129 us (0.13)
  the two profiles are of different devices: /device:TPU:18 before, /device:TPU:1 now
where the time goes in v1:
time: 129 us
  waiting for transfers between devices  45.2 us (35%)
  starting transfers between devices  37.7 us (29%)
  Pallas kernels  24.4 us (19%)
  local copies, waits for them, and re-layouts  14.5 us (11%)
  other arithmetic  5.95 us (5%)
  between operations  1.49 us (1%)
    ppermute x11, starting transfers between devices, swapped(): lax.ppermute(value, axis, [(source, source ^ bit) for source in range(cou...  28.9 us
    pallas_call x1, Pallas kernels, all_windows(): pl.pallas_call(functools.partial(flat_kernel, size, modes, slots, tile),...  24.4 us
    ppermute x2, waiting for transfers between devices, shifted(): lax.ppermute(value, axis, [(source, source + steps) for source in range(f...  20.8 us
    ppermute x11, waiting for transfers between devices, swapped(): lax.ppermute(value, axis, [(source, source ^ bit) for source in range(cou...  19.9 us
    unnamed x30, local copies, waits for them, and re-layouts  13 us
    ppermute x2, starting transfers between devices, shifted(): lax.ppermute(value, axis, [(source, source + steps) for source in range(f...  5.9 us
    ppermute x1, waiting for transfers between devices, shards(): lax.ppermute(halo, 'scan', [(s, s + 1) for s in range(1, count - 1, 2)])  4.59 us
    ppermute x1, starting transfers between devices, shards(): lax.ppermute(halo, 'scan', [(s, s + 1) for s in range(1, count - 1, 2)])  2.9 us
  transfers between devices with their start and end apart: 14, of which 10 were waited for; matrix products, arithmetic and copies ran while one was open for 10% of the time, Pallas kernels for 0%

profile of v1, /device:TPU:1, one launch (start us, length us, event | category | flops | bytes accessed | tf_op | source)
XLA Modules:
  0.0 129.2 jit_solution(4906141353786051923)
XLA Ops:
  1.4 0.8 copy.22
  2.2 1.1 constant_dynamic-update-slice_fusion.9
  3.4 0.9 copy-done.8
  4.3 1.1 pad_maximum_fusion.refs_4_
  5.3 4.6 %collective-permute-start = (f32[1032,128]{1,0:T(8,128)S(1)}, f32[1032,128]{1,0:T(8,128)S(1)}, u32[]{:S(2)}, u32[]{:S(2)}) collective-permute-start(f32[1032,128]{1,0:T(8,128)S(1)} %pad_maximum_fusion.refs_4_), channel_id=1, source_target_pairs={{0,2},{1,3},{2,4},{3,5},{4,6},{5,7},{6,8},{7,9},{8,10},{9,11},{10,... | collective-permute-start | bytes 1585160 | tf_op jit(solution)/shard_map/ppermute | solution.py:20
  10.0 1.2 slice_select_fusion
  16.1 1.3 collective-permute-start.4
  17.4 20.8 %collective-permute-done.refs_6_ = f32[1032,128]{1,0:T(8,128)S(1)} collective-permute-done((f32[1032,128]{1,0:T(8,128)S(1)}, f32[1032,128]{1,0:T(8,128)S(1)}, u32[]{:S(2)}, u32[]{:S(2)}) %collective-permute-start) | collective-permute-done | bytes 528416 | tf_op jit(solution)/shard_map/ppermute | solution.py:20
  38.2 0.9 collective-permute-start.1
  41.5 1.0 collective-permute-done.5.refs_9_
  42.6 0.9 copy-done.7
  43.4 1.0 copy-done
  44.5 1.0 copy-done.1
  45.5 1.0 copy-done.2
  46.5 1.0 copy-done.3
  47.5 1.0 copy-done.4
  48.5 24.4 %shard_map.121 = (f32[2,2,256,256]{3,2,1,0:T(8,128)}, f32[2,2,384,256]{3,2,1,0:T(8,128)}, f32[1056,128]{1,0:T(8,128)S(1)}) custom-call(s32[3]{0:T(128)S(1)} %pad_add_fusion.refs_0_, s32[48,3]{1,0:T(8,128)S(1)} %convert_element_type.22.refs_1_, f32[2,2,256,256]{3,2,1,0:T(8,128)} %refs_2_.1, f32[2,2,256,256]{3,2,1,0:T(8,128)} %copy-done.5, ...), custom_call_target="tpu_custom_call" | custom-call | tf_op jit(solution)/shard_map/pallas_call | solution.py:244
  72.9 5.2 %collective-permute-start.8 = (f32[528,128]{1,0:T(8,128)S(1)}, f32[528,128]{1,0:T(8,128)S(1)}, u32[]{:S(2)}, u32[]{:S(2)}) collective-permute-start(f32[528,128]{1,0:T(8,128)S(1)} %constant_dynamic-slice_fusion.1), channel_id=1, source_target_pairs={{0,1},{1,0},{2,3},{3,2},{4,5},{5,4},{6,7},{7,6},{8,9},{9,8},{10,11... | collective-permute-start | bytes 811016 | tf_op jit(solution)/shard_map/ppermute | solution.py:25
  78.2 1.1 collective-permute-done.8
  79.4 2.2 %collective-permute-start.9 = (f32[264,128]{1,0:T(8,128)S(1)}, f32[264,128]{1,0:T(8,128)S(1)}, u32[]{:S(2)}, u32[]{:S(2)}) collective-permute-start(f32[264,128]{1,0:T(8,128)S(1)} %constant_dynamic-slice_fusion), channel_id=1, source_target_pairs={{0,2},{1,3},{2,0},{3,1},{4,6},{5,7},{6,4},{7,5},{8,10},{9,11},{10,... | collective-permute-start | bytes 405512 | tf_op jit(solution)/shard_map/ppermute | solution.py:25
  81.6 3.7 %collective-permute-done.9 = f32[264,128]{1,0:T(8,128)S(1)} collective-permute-done((f32[264,128]{1,0:T(8,128)S(1)}, f32[264,128]{1,0:T(8,128)S(1)}, u32[]{:S(2)}, u32[]{:S(2)}) %collective-permute-start.9) | collective-permute-done | bytes 135200 | tf_op jit(solution)/shard_map/ppermute | solution.py:25
  85.9 3.6 %collective-permute-done.10 = f32[264,128]{1,0:T(8,128)S(1)} collective-permute-done((f32[264,128]{1,0:T(8,128)S(1)}, f32[264,128]{1,0:T(8,128)S(1)}, u32[]{:S(2)}, u32[]{:S(2)}) %collective-permute-start.10) | collective-permute-done | bytes 135200 | tf_op jit(solution)/shard_map/ppermute | solution.py:25
  89.6 15.7 %collective-permute-start.11 = (f32[264,128]{1,0:T(8,128)S(1)}, f32[264,128]{1,0:T(8,128)S(1)}, u32[]{:S(2)}, u32[]{:S(2)}) collective-permute-start(f32[264,128]{1,0:T(8,128)S(1)} %add.64), channel_id=1, source_target_pairs={{0,8},{1,9},{2,10},{3,11},{4,12},{5,13},{6,14},{7,15},{8,0},{9,1},... | collective-permute-start | bytes 405512 | tf_op jit(solution)/shard_map/ppermute | solution.py:25
  105.2 6.4 %collective-permute-done.11 = f32[264,128]{1,0:T(8,128)S(1)} collective-permute-done((f32[264,128]{1,0:T(8,128)S(1)}, f32[264,128]{1,0:T(8,128)S(1)}, u32[]{:S(2)}, u32[]{:S(2)}) %collective-permute-start.11) | collective-permute-done | bytes 135200 | tf_op jit(solution)/shard_map/ppermute | solution.py:25
  111.6 1.2 collective-permute-start.12
  112.8 2.7 %collective-permute-done.12 = f32[264,128]{1,0:T(8,128)S(1)} collective-permute-done((f32[264,128]{1,0:T(8,128)S(1)}, f32[264,128]{1,0:T(8,128)S(1)}, u32[]{:S(2)}, u32[]{:S(2)}) %collective-permute-start.12) | collective-permute-done | bytes 135200 | tf_op jit(solution)/shard_map/ppermute | solution.py:25
  115.6 2.3 %collective-permute-start.13 = (f32[528,128]{1,0:T(8,128)S(1)}, f32[528,128]{1,0:T(8,128)S(1)}, u32[]{:S(2)}, u32[]{:S(2)}) collective-permute-start(f32[528,128]{1,0:T(8,128)S(1)} %pad_maximum_fusion.2), channel_id=1, source_target_pairs={{0,1},{1,0},{2,3},{3,2},{4,5},{5,4},{6,7},{7,6},{8,9},{9,8},{10,11... | collective-permute-start | bytes 811016 | tf_op jit(solution)/shard_map/ppermute | solution.py:25
  117.9 1.2 slice_add_fusion.1
  119.1 2.9 %collective-permute-start.7 = (f32[2,2,128,256]{3,2,1,0:T(8,128)S(1)}, f32[2,2,128,256]{3,2,1,0:T(8,128)S(1)}, u32[]{:S(2)}, u32[]{:S(2)}) collective-permute-start(f32[2,2,128,256]{3,2,1,0:T(8,128)S(1)} %slice_add_fusion.1), channel_id=1, source_target_pairs={{1,2},{3,4},{5,6},{7,8},{9,10},{11,12},{13,14},{17,18},{19,20},{21... | collective-permute-start | bytes 1572872 | tf_op jit(solution)/shard_map/ppermute | solution.py:323
  122.7 0.8 pad_maximum_fusion.1
  123.5 4.6 %collective-permute-done.7 = f32[2,2,128,256]{3,2,1,0:T(8,128)S(1)} collective-permute-done((f32[2,2,128,256]{3,2,1,0:T(8,128)S(1)}, f32[2,2,128,256]{3,2,1,0:T(8,128)S(1)}, u32[]{:S(2)}, u32[]{:S(2)}) %collective-permute-start.7) | collective-permute-done | bytes 524320 | tf_op jit(solution)/shard_map/ppermute | solution.py:323
  128.1 1.1 fusion
  (56 shorter events, 9.2 us)
Async XLA Ops:
  0.6 9.4 %collective-permute-start.3 = (f32[2,2,256,256]{3,2,1,0:T(8,128)}, f32[2,2,256,256]{3,2,1,0:T(8,128)S(1)}, u32[]{:S(2)}, u32[]{:S(2)}) collective-permute-start(f32[2,2,256,256]{3,2,1,0:T(8,128)} %refs_2_.1), channel_id=1, source_target_pairs={{0,1},{1,0},{2,3},{3,2},{4,5},{5,4},{6,7},{7,6},{8,9},{9,8},{10,11... | collective-permute-start | bytes 3145736 | tf_op jit(solution)/shard_map/ppermute | solution.py:25
  2.2 36.9 %copy-start.9 = (f32[128,128]{1,0:T(8,128)S(1)}, f32[128,128]{1,0:T(8,128)}, u32[]{:S(2)}) copy-start(f32[128,128]{1,0:T(8,128)} %param.12) | copy-start | bytes 196612
  3.4 0.9 copy-start.8
  5.3 32.8 %collective-permute-start = (f32[1032,128]{1,0:T(8,128)S(1)}, f32[1032,128]{1,0:T(8,128)S(1)}, u32[]{:S(2)}, u32[]{:S(2)}) collective-permute-start(f32[1032,128]{1,0:T(8,128)S(1)} %pad_maximum_fusion.refs_4_), channel_id=1, source_target_pairs={{0,2},{1,3},{2,4},{3,5},{4,6},{5,7},{6,8},{7,9},{8,10},{9,11},{10,... | collective-permute-start | bytes 1585160 | tf_op jit(solution)/shard_map/ppermute | solution.py:20
  10.0 7.4 %copy-start.5 = (f32[2,2,256,256]{3,2,1,0:T(8,128)}, f32[2,2,256,256]{3,2,1,0:T(8,128)S(1)}, u32[]{:S(2)}) copy-start(f32[2,2,256,256]{3,2,1,0:T(8,128)S(1)} %collective-permute-done.3.refs_3_) | copy-start | bytes 3145732
  16.1 23.3 %collective-permute-start.4 = (f32[1544,128]{1,0:T(8,128)}, f32[1544,128]{1,0:T(8,128)S(1)}, u32[]{:S(2)}, u32[]{:S(2)}) collective-permute-start(f32[1544,128]{1,0:T(8,128)} %constant_dynamic-update-slice_fusion), channel_id=1, source_target_pairs={{2,0},{3,1},{4,2},{5,3},{6,4},{7,5},{8,6},{9,7},{10,8},{11,9},{12,... | collective-permute-start | bytes 2371592 | tf_op jit(solution)/shard_map/ppermute | solution.py:20
  38.2 2.5 %collective-permute-start.1 = (f32[1032,128]{1,0:T(8,128)S(1)}, f32[1032,128]{1,0:T(8,128)S(1)}, u32[]{:S(2)}, u32[]{:S(2)}) collective-permute-start(f32[1032,128]{1,0:T(8,128)S(1)} %collective-permute-done.refs_6_), channel_id=1, source_target_pairs={{0,1},{1,0},{2,3},{3,2},{4,5},{5,4},{6,7},{7,6},{8,9},{9,8},{10,11... | collective-permute-start | bytes 1585160 | tf_op jit(solution)/shard_map/ppermute | solution.py:25
  39.1 2.3 %collective-permute-start.2 = (f32[1032,128]{1,0:T(8,128)S(1)}, f32[1032,128]{1,0:T(8,128)S(1)}, u32[]{:S(2)}, u32[]{:S(2)}) collective-permute-start(f32[1032,128]{1,0:T(8,128)S(1)} %pad_maximum_fusion.refs_4_), channel_id=1, source_target_pairs={{0,1},{1,0},{2,3},{3,2},{4,5},{5,4},{6,7},{7,6},{8,9},{9,8},{10,11... | collective-permute-start | bytes 1585160 | tf_op jit(solution)/shard_map/ppermute | solution.py:25
  39.4 3.1 %collective-permute-start.5 = (f32[1544,128]{1,0:T(8,128)S(1)}, f32[1544,128]{1,0:T(8,128)S(1)}, u32[]{:S(2)}, u32[]{:S(2)}) collective-permute-start(f32[1544,128]{1,0:T(8,128)S(1)} %collective-permute-done.4.refs_8_), channel_id=1, source_target_pairs={{0,1},{1,0},{2,3},{3,2},{4,5},{5,4},{6,7},{7,6},{8,9},{9,8},{10,11... | collective-permute-start | bytes 2371592 | tf_op jit(solution)/shard_map/ppermute | solution.py:25
  42.5 0.9 copy-start.7
  43.4 1.0 copy-start
  44.5 1.0 copy-start.1
  45.5 1.0 copy-start.2
  46.5 1.0 copy-start.3
  47.5 1.0 copy-start.4
  72.9 6.4 %collective-permute-start.8 = (f32[528,128]{1,0:T(8,128)S(1)}, f32[528,128]{1,0:T(8,128)S(1)}, u32[]{:S(2)}, u32[]{:S(2)}) collective-permute-start(f32[528,128]{1,0:T(8,128)S(1)} %constant_dynamic-slice_fusion.1), channel_id=1, source_target_pairs={{0,1},{1,0},{2,3},{3,2},{4,5},{5,4},{6,7},{7,6},{8,9},{9,8},{10,11... | collective-permute-start | bytes 811016 | tf_op jit(solution)/shard_map/ppermute | solution.py:25
  78.1 39.8 %collective-permute-start.6 = (f32[2,2,384,256]{3,2,1,0:T(8,128)}, f32[2,2,384,256]{3,2,1,0:T(8,128)S(1)}, u32[]{:S(2)}, u32[]{:S(2)}) collective-permute-start(f32[2,2,384,256]{3,2,1,0:T(8,128)} %get-tuple-element.7), channel_id=1, source_target_pairs={{0,1},{1,0},{2,3},{3,2},{4,5},{5,4},{6,7},{7,6},{8,9},{9,8},{10,11... | collective-permute-start | bytes 4718600 | tf_op jit(solution)/shard_map/ppermute | solution.py:25
  79.4 5.9 %collective-permute-start.9 = (f32[264,128]{1,0:T(8,128)S(1)}, f32[264,128]{1,0:T(8,128)S(1)}, u32[]{:S(2)}, u32[]{:S(2)}) collective-permute-start(f32[264,128]{1,0:T(8,128)S(1)} %constant_dynamic-slice_fusion), channel_id=1, source_target_pairs={{0,2},{1,3},{2,0},{3,1},{4,6},{5,7},{6,4},{7,5},{8,10},{9,11},{10,... | collective-permute-start | bytes 405512 | tf_op jit(solution)/shard_map/ppermute | solution.py:25
  85.3 4.3 %collective-permute-start.10 = (f32[264,128]{1,0:T(8,128)S(1)}, f32[264,128]{1,0:T(8,128)S(1)}, u32[]{:S(2)}, u32[]{:S(2)}) collective-permute-start(f32[264,128]{1,0:T(8,128)S(1)} %dynamic-slice_add_fusion.1), channel_id=1, source_target_pairs={{0,4},{1,5},{2,6},{3,7},{4,0},{5,1},{6,2},{7,3},{8,12},{9,13},{10,... | collective-permute-start | bytes 405512 | tf_op jit(solution)/shard_map/ppermute | solution.py:25
  89.6 22.0 %collective-permute-start.11 = (f32[264,128]{1,0:T(8,128)S(1)}, f32[264,128]{1,0:T(8,128)S(1)}, u32[]{:S(2)}, u32[]{:S(2)}) collective-permute-start(f32[264,128]{1,0:T(8,128)S(1)} %add.64), channel_id=1, source_target_pairs={{0,8},{1,9},{2,10},{3,11},{4,12},{5,13},{6,14},{7,15},{8,0},{9,1},... | collective-permute-start | bytes 405512 | tf_op jit(solution)/shard_map/ppermute | solution.py:25
  111.6 3.9 %collective-permute-start.12 = (f32[264,128]{1,0:T(8,128)S(1)}, f32[264,128]{1,0:T(8,128)S(1)}, u32[]{:S(2)}, u32[]{:S(2)}) collective-permute-start(f32[264,128]{1,0:T(8,128)S(1)} %add.65), channel_id=1, source_target_pairs={{0,2},{1,3},{2,0},{3,1},{4,6},{5,7},{6,4},{7,5},{8,10},{9,11},{10,... | collective-permute-start | bytes 405512 | tf_op jit(solution)/shard_map/ppermute | solution.py:25
  115.6 6.4 %collective-permute-start.13 = (f32[528,128]{1,0:T(8,128)S(1)}, f32[528,128]{1,0:T(8,128)S(1)}, u32[]{:S(2)}, u32[]{:S(2)}) collective-permute-start(f32[528,128]{1,0:T(8,128)S(1)} %pad_maximum_fusion.2), channel_id=1, source_target_pairs={{0,1},{1,0},{2,3},{3,2},{4,5},{5,4},{6,7},{7,6},{8,9},{9,8},{10,11... | collective-permute-start | bytes 811016 | tf_op jit(solution)/shard_map/ppermute | solution.py:25
  117.9 10.2 %copy-start.6 = (f32[2,2,256,256]{3,2,1,0:T(8,128)S(1)}, f32[2,2,256,256]{3,2,1,0:T(8,128)}, u32[]{:S(2)}) copy-start(f32[2,2,256,256]{3,2,1,0:T(8,128)} %get-tuple-element.6) | copy-start | bytes 3145732
  119.1 9.0 %collective-permute-start.7 = (f32[2,2,128,256]{3,2,1,0:T(8,128)S(1)}, f32[2,2,128,256]{3,2,1,0:T(8,128)S(1)}, u32[]{:S(2)}, u32[]{:S(2)}) collective-permute-start(f32[2,2,128,256]{3,2,1,0:T(8,128)S(1)} %slice_add_fusion.1), channel_id=1, source_target_pairs={{1,2},{3,4},{5,6},{7,8},{9,10},{11,12},{13,14},{17,18},{19,20},{21... | collective-permute-start | bytes 1572872 | tf_op jit(solution)/shard_map/ppermute | solution.py:323
